TPU v7x, 32 devices: a whole 2x2x4 slice. The times are simulated.
32 devices in a mesh: dom: 8 (over z, x), feat: 4 (over y, core).
Axes of the slice: x: 2, y: 2, z: 4, core: 2. Of those that a mesh axis runs over, the one named last changes fastest.
Arguments:
- features: bfloat16 [768, 16384], P('feat', 'dom'), may hold values from -6 to 6
- neighbors: int32 [16, 16384], P(None, 'dom'), may hold values from 0 to 3071
- degree: int32 [16384], P('dom'), may hold values from 1 to 16
- send_rows: int32 [8, 8, 128], P('dom'), may hold values from 0 to 2047
- labels: int32 [16384], P('dom'), may hold values from 0 to 1
- w_self: bfloat16 [768, 512], replicated, may hold values from -0.21875 to 0.21875
- w_neigh: bfloat16 [768, 512], replicated, may hold values from -0.21875 to 0.21875
- bias: float32 [512], replicated, may hold values from -3 to 3
- a_self: float32 [512], replicated, may hold values from -0.5 to 0.5
- a_neigh: float32 [512], replicated, may hold values from -0.5 to 0.5
Outputs:
- logits: float32 [16384], P('dom')
- grad_self: float32 [768, 512], P('feat')
- grad_neigh: float32 [768, 512], P('feat')
Inputs may be any that keep to these rules, and one draw needn't show every extreme that they name: `neighbors`: slots under 2048 are the partition's own nodes, the others nodes sent by other partitions.
All inputs are finite; a program needn't handle non-finite values.
Results may differ from a plain program's by a relative error of at most 0.012.
The roundings to bfloat16 on the way count: a program that leaves them out, or rounds other values in their place, can miss the bound.
Values may be sent and summed in bfloat16 or wider, within the bound.
A program may use at most 128 MiB of HBM per device.

v0:
```python
import functools

import jax
import jax.numpy as jnp
from jax import lax
from jax.experimental import pallas as pl
from jax.experimental.pallas import tpu as pltpu
from jax.sharding import PartitionSpec as P

MESH = pl.DeviceIdType.MESH
BF = jnp.bfloat16
F32 = jnp.float32
NN = (((1,), (0,)), ((), ()))
NT = (((1,), (1,)), ((), ()))
TN = (((0,), (0,)), ((), ()))
GROUPS = 6
BITS = 5


def dot(a, b, dims):
    return lax.dot_general(a, b, dims, preferred_element_type=F32)


def split(row):
    wide = jnp.broadcast_to(row, (16, row.shape[1]))
    sub = lax.broadcasted_iota(jnp.int32, wide.shape, 0)
    first = wide.astype(BF).astype(F32)
    rest = wide - first
    second = rest.astype(BF).astype(F32)
    third = rest - second
    out = jnp.where(sub == 0, first, jnp.where(sub == 1, second, jnp.where(sub == 2, third, 0.0)))
    return out.astype(BF)


def total(rows):
    return jnp.sum(rows, axis=0, keepdims=True)


def kernel(
    parts, slices, reduce_here, scale,
    *refs,
):
    inputs, refs = refs[:10], refs[10:]
    held, refs = refs[3:13], refs[:3] + refs[13:]
    run(parts, slices, reduce_here, scale, inputs, held, *refs)


def run(
    parts, slices, reduce_here, scale, inputs, held,
    logit_ref, gself_ref, gneigh_ref,
    hi_ref, val_ref, count_ref, pick_ref, fblk_ref, ablk_ref, agg_ref, out_ref, inc_ref, inctab_ref,
    col_ref, pre_ref, mask_ref, score_ref, srow_ref, sout_ref, sin_ref, stab_ref, wsplit_ref, slot_ref,
    gout_ref, gin_ref, back_ref, dn_ref, dl_ref, acc_ref, dpre_ref, rs_out, rs_in, ag_ref,
    feat_send, feat_recv, dom_send, dom_recv, load_sem,
):
    feat_ref, neigh_ref, degree_ref, send_ref, label_ref, ws_ref, wn_ref, bias_ref, as_ref, an_ref = held
    loads = [pltpu.make_async_copy(a, b, load_sem.at[k]) for k, (a, b) in enumerate(zip(inputs, held))]
    for k in (0, 3, 1, 2, 5, 7, 8, 9, 6, 4):
        loads[k].start()
    d = lax.axis_index("dom")
    f = lax.axis_index("feat")
    cols, nodes = feat_ref.shape
    fan = neigh_ref.shape[0]
    each = send_ref.shape[1]
    remote = parts * each
    table = nodes + remote
    block = nodes // slices
    hid = ws_ref.shape[1]
    rows = table // GROUPS
    shift = rows.bit_length() - 1

    chips = slices // 2
    chip, core = f // 2, lax.rem(f, 2)

    def feat_peer(j):
        return 2 * lax.rem(chip + j // 2, chips) + lax.rem(core + j % 2, 2)

    def feat_from(j):
        return 2 * lax.rem(chip + chips - j // 2, chips) + lax.rem(core + j % 2, 2)

    far_first = list(range(2, slices)) + [1]

    barrier = pltpu.get_barrier_semaphore()
    for j in range(1, parts):
        pl.semaphore_signal(barrier, inc=1, device_id={"dom": lax.rem(d + j, parts)}, device_id_type=MESH)
    for j in range(1, slices):
        pl.semaphore_signal(barrier, inc=1, device_id={"feat": feat_peer(j)}, device_id_type=MESH)
    pl.semaphore_wait(barrier, parts + slices - 2)

    sent = []

    def feat_copy(phase, j, src, dst):
        copy = pltpu.make_async_remote_copy(
            src_ref=src, dst_ref=dst, send_sem=feat_send.at[phase, j], recv_sem=feat_recv.at[phase, j],
            device_id={"feat": feat_peer(j)}, device_id_type=MESH)
        copy.start()
        sent.append(copy)

    def dom_copy(phase, j, src, dst):
        copy = pltpu.make_async_remote_copy(
            src_ref=src, dst_ref=dst, send_sem=dom_send.at[phase, j], recv_sem=dom_recv.at[phase, j],
            device_id={"dom": lax.rem(d + j, parts)}, device_id_type=MESH)
        copy.start()
        sent.append(copy)

    def forward(phase, j, src, dst):
        copy = pltpu.make_async_remote_copy(
            src_ref=src, dst_ref=dst, send_sem=feat_send.at[phase, j], recv_sem=feat_recv.at[phase, j],
            device_id={"feat": feat_peer(1)}, device_id_type=MESH)
        copy.start()
        sent.append(copy)

    def feat_wait(phase, j, dst):
        pltpu.make_async_remote_copy(
            src_ref=dst, dst_ref=dst, send_sem=feat_send.at[phase, j], recv_sem=feat_recv.at[phase, j],
            device_id={"feat": feat_peer(j)}, device_id_type=MESH).wait_recv()

    def dom_wait(phase, j, dst):
        pltpu.make_async_remote_copy(
            src_ref=dst, dst_ref=dst, send_sem=dom_send.at[phase, j], recv_sem=dom_recv.at[phase, j],
            device_id={"dom": lax.rem(d + j, parts)}, device_id_type=MESH).wait_recv()

    def dom_peer(j):
        return lax.rem(d + j, parts)

    def dom_from(j):
        return lax.rem(d + parts - j, parts)

    def span(index):
        return pl.ds(pl.multiple_of(index * block, block), block)

    loads[0].wait()
    loads[3].wait()

    def pick(i, _):
        r = pl.multiple_of(i * 256, 256)
        here = lax.broadcasted_iota(jnp.int32, (256, each), 0) + r
        for p in range(parts):
            pick_ref[pl.ds(r, 256), p * each:(p + 1) * each] = jnp.where(here == send_ref[p:p + 1, :], 1.0, 0.0).astype(BF)
        return 0

    lax.fori_loop(0, nodes // 256, pick, 0)
    step = min(256, remote)
    for c in range(remote // step):
        got = dot(feat_ref[...], pick_ref[:, c * step:(c + 1) * step], NN).astype(BF)
        for p in range(step // each):
            out_ref[c * (step // each) + p] = got[:, p * each:(p + 1) * each]
    for j in range(1, parts):
        dom_copy(0, j, out_ref.at[dom_peer(j)], inc_ref.at[d])
    inc_ref[d] = out_ref[d]

    for j in far_first:
        feat_copy(0, j, feat_ref.at[:, span(feat_peer(j))], fblk_ref.at[f])
    fblk_ref[f] = feat_ref[:, span(f)]

    loads[1].wait()
    loads[2].wait()
    slot = lax.broadcasted_iota(jnp.int32, (fan, nodes), 0)
    used = slot < degree_ref[...]
    hi_ref[...] = neigh_ref[...] & (rows - 1)
    val_ref[...] = jnp.where(used, jnp.left_shift(jnp.int32(1), (neigh_ref[...] >> shift) * BITS), 0)

    def count_lanes(c, first):
        lanes = pl.ds(pl.multiple_of(first + c * 128, 128), 128)
        his = [jnp.broadcast_to(hi_ref[k:k + 1, lanes], (16, 128)) for k in range(fan)]
        vals = [jnp.broadcast_to(val_ref[k:k + 1, lanes], (16, 128)) for k in range(fan)]
        base = lax.broadcasted_iota(jnp.int32, (16, 128), 0)

        def count_rows(i, _):
            r = pl.multiple_of(i * 16, 16)
            here = base + r
            terms = [jnp.where(h == here, v, 0) for h, v in zip(his, vals)]
            while len(terms) > 1:
                terms = [a + b for a, b in zip(terms[::2], terms[1::2])] + terms[len(terms) & ~1:]
            word = terms[0]
            for g in range(GROUPS):
                part = (word >> (BITS * g)) & ((1 << BITS) - 1)
                count_ref[pl.ds(pl.multiple_of(g * rows + r, 16), 16), lanes] = part.astype(F32).astype(BF)
            return 0

        lax.fori_loop(0, rows // 16, count_rows, 0)
        return first

    def count_block(index):
        lax.fori_loop(0, block // 128, count_lanes, index * block)

    for j in far_first:
        count_block(feat_peer(j))
    inverse = 1.0 / degree_ref[...].astype(F32)

    for k in (7, 8, 9):
        loads[k].wait()
    for k, ref in enumerate((bias_ref, as_ref, an_ref)):
        col_ref[k] = jnp.broadcast_to(ref[...], (128, hid)).T

    for j in range(1, parts):
        dom_wait(0, j, inc_ref.at[dom_from(j)])
    for p in range(parts):
        inctab_ref[:, p * each:(p + 1) * each] = inc_ref[p]

    tile = min(256, block)

    def aggregate(index):
        for t in range(block // tile):
            lanes = pl.ds(pl.multiple_of(index * block + t * tile, tile), tile)
            sums = dot(feat_ref[...], count_ref[:nodes, lanes], NN)
            sums = sums + dot(inctab_ref[...], count_ref[nodes:, lanes], NN)
            agg_ref[:, lanes] = (sums * (1.0 / degree_ref[:, lanes].astype(F32))).astype(BF)

    for j in far_first:
        aggregate(feat_peer(j))
        feat_copy(1, j, agg_ref.at[:, span(feat_peer(j))], ablk_ref.at[f])
    count_block(f)
    aggregate(f)
    ablk_ref[f] = agg_ref[:, span(f)]

    for j in range(1, slices):
        feat_wait(0, j, fblk_ref.at[feat_from(j)])
    depth = slices * cols
    loads[5].wait()
    pre_ref[...] = dot(ws_ref[...], fblk_ref[...].reshape(depth, block), TN)
    for j in range(1, slices):
        feat_wait(1, j, ablk_ref.at[feat_from(j)])
    loads[6].wait()
    pre_ref[...] += dot(wn_ref[...], ablk_ref[...].reshape(depth, block), TN)
    for t in range(block // 128):
        pre = pre_ref[:, t * 128:(t + 1) * 128] + col_ref[0]
        hidden = jnp.maximum(pre, 0.0)
        mask_ref[f, :, t * 128:(t + 1) * 128] = jnp.where(pre > 0, 1.0, 0.0).astype(BF)
        own = jnp.broadcast_to(total(hidden * col_ref[1]), (8, 128))
        other = jnp.broadcast_to(total(hidden * col_ref[2]), (8, 128))
        sub = lax.broadcasted_iota(jnp.int32, (8, 128), 0)
        score_ref[f, :, t * 128:(t + 1) * 128] = jnp.where(sub == 0, own, other)
    for j in far_first:
        feat_copy(2, j, score_ref.at[f], score_ref.at[f])
    for j in range(2, slices, 2):
        feat_copy(3, j, mask_ref.at[f], mask_ref.at[f])
    feat_copy(3, 1, mask_ref.at[f], mask_ref.at[f])

    for j in range(1, slices):
        feat_wait(2, j, score_ref.at[feat_from(j)])
    for s in range(slices):
        srow_ref[:, s * block:(s + 1) * block] = score_ref[s]
    own_score = split(srow_ref[1:2, :])
    boundary = total(dot(own_score, pick_ref[...], NN))
    for p in range(parts):
        sout_ref[p] = jnp.broadcast_to(boundary[:, p * each:(p + 1) * each], (8, each))
    for j in range(1, parts):
        dom_copy(1, j, sout_ref.at[dom_peer(j)], sin_ref.at[d])
    sin_ref[d] = sout_ref[d]

    def own_tile(i, _):
        lanes = pl.ds(pl.multiple_of(i * 256, 256), 256)
        slot_ref[0:1, lanes] = total(dot(own_score, count_ref[:nodes, lanes], NN))
        return 0

    lax.fori_loop(0, nodes // 256, own_tile, 0)
    for j in range(1, parts):
        dom_wait(1, j, sin_ref.at[dom_from(j)])
    for p in range(parts):
        stab_ref[:, p * each:(p + 1) * each] = sin_ref[p]
    spread = split(stab_ref[0:1, :])

    def logit_tile(i, _):
        lanes = pl.ds(pl.multiple_of(i * 256, 256), 256)
        slot_ref[0:1, lanes] += total(dot(spread, count_ref[nodes:, lanes], NN))
        return 0

    lax.fori_loop(0, nodes // 256, logit_tile, 0)
    logits = srow_ref[0:1, :] + slot_ref[0:1, :nodes] * inverse
    logit_ref[...] = logits
    loads[4].wait()
    dlogit = (1.0 / (1.0 + jnp.exp(-logits)) - label_ref[...].astype(F32)) * scale
    dl_ref[...] = dlogit
    wsplit_ref[...] = split(dlogit * inverse)

    def slot_tile(i, _):
        lanes = pl.ds(pl.multiple_of(i * 256, 256), 256)
        slot_ref[0:1, lanes] = total(dot(wsplit_ref[...], count_ref[lanes, :], NT))
        return 0

    lax.fori_loop(nodes // 256, table // 256, slot_tile, 0)
    for p in range(parts):
        gout_ref[p] = jnp.broadcast_to(slot_ref[0:1, nodes + p * each:nodes + (p + 1) * each], (8, each))
    for j in range(1, parts):
        dom_copy(2, j, gout_ref.at[dom_peer(j)], gin_ref.at[d])
    gin_ref[d] = gout_ref[d]
    lax.fori_loop(0, nodes // 256, slot_tile, 0)

    for j in range(2, slices, 2):
        feat_wait(3, j, mask_ref.at[feat_from(j)])
        index = feat_from(j)
        forward(3, j + 1, mask_ref.at[index], mask_ref.at[index])

    for j in range(1, parts):
        dom_wait(2, j, gin_ref.at[dom_from(j)])
    for p in range(parts):
        back_ref[:, p * each:(p + 1) * each] = gin_ref[p]
    returned = split(back_ref[0:1, :])

    def back_tile(i, _):
        lanes = pl.ds(pl.multiple_of(i * 256, 256), 256)
        dn_ref[0:1, lanes] = slot_ref[0:1, lanes] + total(dot(returned, pick_ref[lanes, :], NT))
        return 0

    lax.fori_loop(0, nodes // 256, back_tile, 0)

    for j in range(slices):
        index = feat_from(j)
        if j % 2:
            feat_wait(3, j, mask_ref.at[index])
        for t in range(block // 128):
            lanes = pl.ds(pl.multiple_of(index * block + t * 128, 128), 128)
            grad = dl_ref[:, lanes] * col_ref[1] + dn_ref[0:1, lanes] * col_ref[2]
            keep = mask_ref[index, :, t * 128:(t + 1) * 128].astype(F32)
            dpre_ref[j, :, t * 128:(t + 1) * 128] = jnp.where(keep > 0, grad, 0.0).astype(BF)
        own = dot(feat_ref[:, span(index)], dpre_ref[j], NT)
        acc_ref[0] = acc_ref[0] + own if j else own

    half = hid // 2
    share = 2 * cols // parts
    spots = [(slice(p // 2 * share, (p // 2 + 1) * share), slice(p % 2 * half, (p % 2 + 1) * half)) for p in range(parts)]

    def send_shares(h):
        for p in range(parts):
            rs_out[h, p] = acc_ref[h, spots[p][0], spots[p][1]].astype(BF)
        for j in range(1, parts):
            dom_copy(3 + h, j, rs_out.at[h, dom_peer(j)], rs_in.at[h, d])

    if reduce_here:
        send_shares(0)
    for j in range(slices):
        other = dot(agg_ref[:, span(feat_from(j))], dpre_ref[j], NT)
        acc_ref[1] = acc_ref[1] + other if j else other
    if reduce_here:
        send_shares(1)
        side = lax.rem(d, 2)
        beside = d + 1 - 2 * side

        def hand_over(h, j, index):
            copy = pltpu.make_async_remote_copy(
                src_ref=ag_ref.at[h, index], dst_ref=ag_ref.at[h, index],
                send_sem=dom_send.at[5 + h, j], recv_sem=dom_recv.at[5 + h, j],
                device_id={"dom": beside}, device_id_type=MESH)
            copy.start()
            sent.append(copy)

        for h in range(2):
            whole = rs_out[h, d].astype(F32)
            for j in range(1, parts):
                dom_wait(3 + h, j, rs_in.at[h, dom_from(j)])
                whole = whole + rs_in[h, dom_from(j)].astype(F32)
            ag_ref[h, d] = whole.astype(BF)
            for j in range(2, parts, 2):
                dom_copy(5 + h, j, ag_ref.at[h, d], ag_ref.at[h, d])
            hand_over(h, 1, d)
        for h in range(2):
            for j in range(2, parts, 2):
                dom_wait(5 + h, j, ag_ref.at[h, dom_from(j)])
                hand_over(h, j + 1, dom_from(j))
        for h, ref in enumerate((gself_ref, gneigh_ref)):
            for j in range(1, parts, 2):
                dom_wait(5 + h, j, ag_ref.at[h, lax.rem(beside + parts + 1 - j, parts)])
            for p in range(parts):
                ref[spots[p][0], spots[p][1]] = ag_ref[h, p].astype(F32)
    else:
        gself_ref[...] = acc_ref[0]
        gneigh_ref[...] = acc_ref[1]
    for copy in sent:
        copy.wait_send()


def body(features, neighbors, degree, send_rows, labels, w_self, w_neigh, bias, a_self, a_neigh):
    parts = lax.axis_size("dom")
    slices = lax.axis_size("feat")
    cols, nodes = features.shape
    fan = neighbors.shape[0]
    each = send_rows.shape[2]
    remote = parts * each
    table = nodes + remote
    block = nodes // slices
    hid = w_self.shape[1]
    share = 2 * cols // parts
    reduce_here = parts % 2 == 0 and share * parts == 2 * cols and share % 16 == 0 and hid % 256 == 0
    scale = float(nodes * parts) ** (-0.5)
    spare = share if reduce_here else 16
    V = pltpu.VMEM
    held = [
        V((cols, nodes), BF), V((fan, nodes), jnp.int32), V((1, nodes), jnp.int32), V((parts, each), jnp.int32),
        V((1, nodes), jnp.int32), V(w_self.shape, BF), V(w_neigh.shape, BF),
        V((1, hid), F32), V((1, hid), F32), V((1, hid), F32),
    ]
    scratch = held + [
        V((fan, nodes), jnp.int32), V((fan, nodes), jnp.int32),
        V((table, nodes), BF), V((nodes, remote), BF),
        V((slices, cols, block), BF), V((slices, cols, block), BF), V((cols, nodes), BF),
        V((parts, cols, each), BF), V((parts, cols, each), BF), V((cols, remote), BF),
        V((3, hid, 128), F32), V((hid, block), F32), V((slices, hid, block), BF),
        V((slices, 8, block), F32), V((8, nodes), F32),
        V((parts, 8, each), F32), V((parts, 8, each), F32), V((8, remote), F32),
        V((16, nodes), BF), V((8, table), F32),
        V((parts, 8, each), F32), V((parts, 8, each), F32), V((8, remote), F32),
        V((8, nodes), F32), V((1, nodes), F32),
        V((2, cols, hid), F32), V((slices, hid, block), BF),
        V((2, parts, spare, hid // 2), BF), V((2, parts, spare, hid // 2), BF), V((2, parts, spare, hid // 2), BF),
        pltpu.SemaphoreType.DMA((4, slices)), pltpu.SemaphoreType.DMA((4, slices)),
        pltpu.SemaphoreType.DMA((7, parts)), pltpu.SemaphoreType.DMA((7, parts)),
        pltpu.SemaphoreType.DMA((10,)),
    ]
    vm = pl.BlockSpec(memory_space=pltpu.VMEM)
    logits, grad_self, grad_neigh = pl.pallas_call(
        functools.partial(kernel, parts, slices, reduce_here, scale),
        out_shape=(
            jax.ShapeDtypeStruct((1, nodes), F32),
            jax.ShapeDtypeStruct((cols, hid), F32),
            jax.ShapeDtypeStruct((cols, hid), F32),
        ),
        in_specs=[pl.BlockSpec(memory_space=pltpu.HBM)] * 10,
        out_specs=(vm, vm, vm),
        scratch_shapes=scratch,
        compiler_params=pltpu.CompilerParams(
            collective_id=0, has_side_effects=True, vmem_limit_bytes=62 * 1024 * 1024),
    )(
        features, neighbors, degree.reshape(1, nodes), send_rows.reshape(parts, each), labels.reshape(1, nodes),
        w_self, w_neigh, bias.reshape(1, hid), a_self.reshape(1, hid), a_neigh.reshape(1, hid),
    )
    if not reduce_here:
        grad_self, grad_neigh = lax.psum((grad_self, grad_neigh), "dom")
    return (logits.reshape(nodes), grad_self, grad_neigh)


def solution(mesh):
    return jax.shard_map(
        body,
        mesh=mesh,
        in_specs=(
            P("feat", "dom"), P(None, "dom"), P("dom"), P("dom", None, None), P("dom"),
            P(), P(), P(), P(), P(),
        ),
        out_specs=(P("dom"), P("feat", None), P("feat", None)),
        check_vma=False,
    )
```

profile of v0, /device:TPU:0, one launch (start us, length us, event | category | flops | bytes accessed | tf_op | source)
XLA Modules:
  0.0 74.5 jit_solution(14310902275338403381)
XLA Ops:
  0.6 70.0 %shard_map.121 = (f32[1,2048]{1,0:T(1,128)}, f32[192,512]{1,0:T(8,128)}, f32[192,512]{1,0:T(8,128)}) custom-call(bf16[192,2048]{1,0:T(8,128)(2,1)} %refs_0_.1, s32[16,2048]{1,0:T(8,128)} %refs_1_.1, s32[1,2048]{1,0:T(1,128)} %bitcast.7, s32[8,128]{1,0:T(8,128)} %bitcast.10, s32[1,2048]{1,0:T(1,128)} %bitcast.8, bf16[768,512]{1,0:T(8,128)(2,1)} %refs_5_.1, ...), custom_call_target="tpu_custom_call" | custom-call | tf_op jit(solution)/shard_map/pallas_call | solution.py:411
  70.6 1.3 %copy.16 = f32[2048]{0:T(1024)} copy(f32[2048]{0:T(1024)} %bitcast.9) | data formatting | bytes 16384
  71.9 0.0 copy-start
  71.9 1.8 %copy.17 = f32[192,512]{1,0:T(8,128)} copy(f32[192,512]{1,0:T(8,128)} %get-tuple-element.13) | data formatting | bytes 786432
  73.7 0.0 copy-done
  73.8 0.7 %copy.18 = f32[192,512]{1,0:T(8,128)} copy(f32[192,512]{1,0:T(8,128)S(1)} %copy-done) | data formatting | bytes 786432
Async XLA Ops:
  71.9 1.8 %copy-start = (f32[192,512]{1,0:T(8,128)S(1)}, f32[192,512]{1,0:T(8,128)}, u32[]{:S(2)}) copy-start(f32[192,512]{1,0:T(8,128)} %get-tuple-element.14) | copy-start | bytes 1179652
where the time goes:
time: 74.7 us; the launch traced here: 74.5 us
  Pallas kernels  70 us (94%)
  local copies, waits for them, and re-layouts  3.86 us (5%)
    pallas_call x1, Pallas kernels, body(): pl.pallas_call(functools.partial(kernel, parts, slices, reduce_here, scal...  70 us
    unnamed x5, local copies, waits for them, and re-layouts  3.86 us

commit v1 on v0

--- a/solution.py
+++ b/solution.py
@@ -12,7 +12,6 @@
 F32 = jnp.float32
 NN = (((1,), (0,)), ((), ()))
 NT = (((1,), (1,)), ((), ()))
-TN = (((0,), (0,)), ((), ()))
 GROUPS = 6
 BITS = 5
 
@@ -50,7 +49,7 @@
     logit_ref, gself_ref, gneigh_ref,
     hi_ref, val_ref, count_ref, pick_ref, fblk_ref, ablk_ref, agg_ref, out_ref, inc_ref, inctab_ref,
     col_ref, pre_ref, mask_ref, score_ref, srow_ref, sout_ref, sin_ref, stab_ref, wsplit_ref, slot_ref,
-    gout_ref, gin_ref, back_ref, dn_ref, dl_ref, acc_ref, dpre_ref, rs_out, rs_in, ag_ref,
+    gout_ref, gin_ref, back_ref, dn_ref, dl_ref, acc_ref, dpre_ref, rs_out, rs_in, ag_ref, wt_ref,
     feat_send, feat_recv, dom_send, dom_recv, load_sem,
 ):
     feat_ref, neigh_ref, degree_ref, send_ref, label_ref, ws_ref, wn_ref, bias_ref, as_ref, an_ref = held
@@ -85,7 +84,6 @@
         pl.semaphore_signal(barrier, inc=1, device_id={"dom": lax.rem(d + j, parts)}, device_id_type=MESH)
     for j in range(1, slices):
         pl.semaphore_signal(barrier, inc=1, device_id={"feat": feat_peer(j)}, device_id_type=MESH)
-    pl.semaphore_wait(barrier, parts + slices - 2)
 
     sent = []
 
@@ -145,6 +143,7 @@
         got = dot(feat_ref[...], pick_ref[:, c * step:(c + 1) * step], NN).astype(BF)
         for p in range(step // each):
             out_ref[c * (step // each) + p] = got[:, p * each:(p + 1) * each]
+    pl.semaphore_wait(barrier, parts + slices - 2)
     for j in range(1, parts):
         dom_copy(0, j, out_ref.at[dom_peer(j)], inc_ref.at[d])
     inc_ref[d] = out_ref[d]
@@ -162,23 +161,28 @@
 
     def count_lanes(c, first):
         lanes = pl.ds(pl.multiple_of(first + c * 128, 128), 128)
-        his = [jnp.broadcast_to(hi_ref[k:k + 1, lanes], (16, 128)) for k in range(fan)]
-        vals = [jnp.broadcast_to(val_ref[k:k + 1, lanes], (16, 128)) for k in range(fan)]
-        base = lax.broadcasted_iota(jnp.int32, (16, 128), 0)
+        his = [jnp.broadcast_to(hi_ref[k:k + 1, lanes], (8, 128)) for k in range(fan)]
+        vals = [jnp.broadcast_to(val_ref[k:k + 1, lanes], (8, 128)) for k in range(fan)]
+        base = lax.broadcasted_iota(jnp.int32, (8, 128), 0)
 
         def count_rows(i, _):
-            r = pl.multiple_of(i * 16, 16)
-            here = base + r
-            terms = [jnp.where(h == here, v, 0) for h, v in zip(his, vals)]
-            while len(terms) > 1:
-                terms = [a + b for a, b in zip(terms[::2], terms[1::2])] + terms[len(terms) & ~1:]
-            word = terms[0]
-            for g in range(GROUPS):
-                part = (word >> (BITS * g)) & ((1 << BITS) - 1)
-                count_ref[pl.ds(pl.multiple_of(g * rows + r, 16), 16), lanes] = part.astype(F32).astype(BF)
+            for u in range(0, 32, 16):
+                r = pl.multiple_of(i * 32 + u, 16)
+                words = []
+                for here in (base + r, base + (r + 8)):
+                    terms = [jnp.where(h == here, v, 0) for h, v in zip(his, vals)]
+                    while len(terms) > 1:
+                        terms = [a + b for a, b in zip(terms[::2], terms[1::2])] + terms[len(terms) & ~1:]
+                    words.append(terms[0])
+                for g in range(GROUPS):
+                    fields = [w >> (BITS * g) if g else w for w in words]
+                    if g < GROUPS - 1:
+                        fields = [w & ((1 << BITS) - 1) for w in fields]
+                    both = jnp.concatenate([w.astype(F32) for w in fields], axis=0)
+                    count_ref[pl.ds(pl.multiple_of(g * rows + r, 16), 16), lanes] = both.astype(BF)
             return 0
 
-        lax.fori_loop(0, rows // 16, count_rows, 0)
+        lax.fori_loop(0, rows // 32, count_rows, 0)
         return first
 
     def count_block(index):
@@ -218,11 +222,13 @@
         feat_wait(0, j, fblk_ref.at[feat_from(j)])
     depth = slices * cols
     loads[5].wait()
-    pre_ref[...] = dot(ws_ref[...], fblk_ref[...].reshape(depth, block), TN)
+    loads[6].wait()
+    wt_ref[0] = ws_ref[...].T
+    wt_ref[1] = wn_ref[...].T
+    pre_ref[...] = dot(wt_ref[0], fblk_ref[...].reshape(depth, block), NN)
     for j in range(1, slices):
         feat_wait(1, j, ablk_ref.at[feat_from(j)])
-    loads[6].wait()
-    pre_ref[...] += dot(wn_ref[...], ablk_ref[...].reshape(depth, block), TN)
+    pre_ref[...] += dot(wt_ref[1], ablk_ref[...].reshape(depth, block), NN)
     for t in range(block // 128):
         pre = pre_ref[:, t * 128:(t + 1) * 128] + col_ref[0]
         hidden = jnp.maximum(pre, 0.0)
@@ -249,24 +255,24 @@
         dom_copy(1, j, sout_ref.at[dom_peer(j)], sin_ref.at[d])
     sin_ref[d] = sout_ref[d]
 
-    def own_tile(i, _):
-        lanes = pl.ds(pl.multiple_of(i * 256, 256), 256)
+    def own_tile(i):
+        lanes = slice(i * 256, (i + 1) * 256)
         slot_ref[0:1, lanes] = total(dot(own_score, count_ref[:nodes, lanes], NN))
-        return 0
-
-    lax.fori_loop(0, nodes // 256, own_tile, 0)
+
+    for i in range(0, nodes // 256):
+        own_tile(i)
     for j in range(1, parts):
         dom_wait(1, j, sin_ref.at[dom_from(j)])
     for p in range(parts):
         stab_ref[:, p * each:(p + 1) * each] = sin_ref[p]
     spread = split(stab_ref[0:1, :])
 
-    def logit_tile(i, _):
-        lanes = pl.ds(pl.multiple_of(i * 256, 256), 256)
+    def logit_tile(i):
+        lanes = slice(i * 256, (i + 1) * 256)
         slot_ref[0:1, lanes] += total(dot(spread, count_ref[nodes:, lanes], NN))
-        return 0
-
-    lax.fori_loop(0, nodes // 256, logit_tile, 0)
+
+    for i in range(0, nodes // 256):
+        logit_tile(i)
     logits = srow_ref[0:1, :] + slot_ref[0:1, :nodes] * inverse
     logit_ref[...] = logits
     loads[4].wait()
@@ -274,18 +280,19 @@
     dl_ref[...] = dlogit
     wsplit_ref[...] = split(dlogit * inverse)
 
-    def slot_tile(i, _):
-        lanes = pl.ds(pl.multiple_of(i * 256, 256), 256)
+    def slot_tile(i):
+        lanes = slice(i * 256, (i + 1) * 256)
         slot_ref[0:1, lanes] = total(dot(wsplit_ref[...], count_ref[lanes, :], NT))
-        return 0
-
-    lax.fori_loop(nodes // 256, table // 256, slot_tile, 0)
+
+    for i in range(nodes // 256, table // 256):
+        slot_tile(i)
     for p in range(parts):
         gout_ref[p] = jnp.broadcast_to(slot_ref[0:1, nodes + p * each:nodes + (p + 1) * each], (8, each))
     for j in range(1, parts):
         dom_copy(2, j, gout_ref.at[dom_peer(j)], gin_ref.at[d])
     gin_ref[d] = gout_ref[d]
-    lax.fori_loop(0, nodes // 256, slot_tile, 0)
+    for i in range(0, nodes // 256):
+        slot_tile(i)
 
     for j in range(2, slices, 2):
         feat_wait(3, j, mask_ref.at[feat_from(j)])
@@ -298,12 +305,12 @@
         back_ref[:, p * each:(p + 1) * each] = gin_ref[p]
     returned = split(back_ref[0:1, :])
 
-    def back_tile(i, _):
-        lanes = pl.ds(pl.multiple_of(i * 256, 256), 256)
+    def back_tile(i):
+        lanes = slice(i * 256, (i + 1) * 256)
         dn_ref[0:1, lanes] = slot_ref[0:1, lanes] + total(dot(returned, pick_ref[lanes, :], NT))
-        return 0
-
-    lax.fori_loop(0, nodes // 256, back_tile, 0)
+
+    for i in range(0, nodes // 256):
+        back_tile(i)
 
     for j in range(slices):
         index = feat_from(j)
@@ -312,8 +319,7 @@
         for t in range(block // 128):
             lanes = pl.ds(pl.multiple_of(index * block + t * 128, 128), 128)
             grad = dl_ref[:, lanes] * col_ref[1] + dn_ref[0:1, lanes] * col_ref[2]
-            keep = mask_ref[index, :, t * 128:(t + 1) * 128].astype(F32)
-            dpre_ref[j, :, t * 128:(t + 1) * 128] = jnp.where(keep > 0, grad, 0.0).astype(BF)
+            dpre_ref[j, :, t * 128:(t + 1) * 128] = grad.astype(BF) * mask_ref[index, :, t * 128:(t + 1) * 128]
         own = dot(feat_ref[:, span(index)], dpre_ref[j], NT)
         acc_ref[0] = acc_ref[0] + own if j else own
 
@@ -368,6 +374,15 @@
         gneigh_ref[...] = acc_ref[1]
     for copy in sent:
         copy.wait_send()
+
+
+def place(*refs):
+    sems = refs[6]
+    copies = [pltpu.make_async_copy(refs[k], refs[3 + k], sems.at[k]) for k in range(3)]
+    for copy in copies:
+        copy.start()
+    for copy in copies:
+        copy.wait()
 
 
 def body(features, neighbors, degree, send_rows, labels, w_self, w_neigh, bias, a_self, a_neigh):
@@ -403,6 +418,7 @@
         V((8, nodes), F32), V((1, nodes), F32),
         V((2, cols, hid), F32), V((slices, hid, block), BF),
         V((2, parts, spare, hid // 2), BF), V((2, parts, spare, hid // 2), BF), V((2, parts, spare, hid // 2), BF),
+        V((2, hid, w_self.shape[0]), BF),
         pltpu.SemaphoreType.DMA((4, slices)), pltpu.SemaphoreType.DMA((4, slices)),
         pltpu.SemaphoreType.DMA((7, parts)), pltpu.SemaphoreType.DMA((7, parts)),
         pltpu.SemaphoreType.DMA((10,)),
@@ -424,7 +440,17 @@
         features, neighbors, degree.reshape(1, nodes), send_rows.reshape(parts, each), labels.reshape(1, nodes),
         w_self, w_neigh, bias.reshape(1, hid), a_self.reshape(1, hid), a_neigh.reshape(1, hid),
     )
-    if not reduce_here:
+    if reduce_here:
+        hbm = pl.BlockSpec(memory_space=pltpu.HBM)
+        logits, grad_self, grad_neigh = pl.pallas_call(
+            place,
+            out_shape=tuple(jax.ShapeDtypeStruct(x.shape, x.dtype) for x in (logits, grad_self, grad_neigh)),
+            in_specs=[hbm] * 3,
+            out_specs=(hbm, hbm, hbm),
+            scratch_shapes=[pltpu.SemaphoreType.DMA((3,))],
+            compiler_params=pltpu.CompilerParams(vmem_limit_bytes=62 * 1024 * 1024),
+        )(logits, grad_self, grad_neigh)
+    else:
         grad_self, grad_neigh = lax.psum((grad_self, grad_neigh), "dom")
     return (logits.reshape(nodes), grad_self, grad_neigh)
 

time: 74.7 us -> 90.4 us (1.21)
  Pallas kernels: 70 us -> 89.5 us
  local copies, waits for them, and re-layouts: 3.86 us -> 0 us
    pallas_call x0 -> x1, Pallas kernels: none -> 25.2 us  [body(): pl.pallas_call(place, out_shape=tuple((jax.ShapeDtypeStruct(x.shape, x.dt...]
    pallas_call x1, Pallas kernels: 70 us -> 64.3 us  [body(): pl.pallas_call(functools.partial(kernel, parts, slices, reduce_here, scal...]
    unnamed x5 -> x0, local copies, waits for them, and re-layouts: 3.86 us -> none
where the time goes in v1:
time: 90.4 us; the launch traced here: 90.3 us
  Pallas kernels  89.5 us (99%)
    pallas_call x1, Pallas kernels, body(): pl.pallas_call(functools.partial(kernel, parts, slices, reduce_here, scal...  64.3 us
    pallas_call x1, Pallas kernels, body(): pl.pallas_call(place, out_shape=tuple((jax.ShapeDtypeStruct(x.shape, x.dt...  25.2 us

profile of v1, /device:TPU:0, one launch (start us, length us, event | category | flops | bytes accessed | tf_op | source)
XLA Modules:
  0.0 90.3 jit_solution(16906740198832771004)
XLA Ops:
  0.6 64.3 %shard_map.121 = (f32[1,2048]{1,0:T(1,128)}, f32[192,512]{1,0:T(8,128)}, f32[192,512]{1,0:T(8,128)}) custom-call(bf16[192,2048]{1,0:T(8,128)(2,1)} %refs_0_.1, s32[16,2048]{1,0:T(8,128)} %refs_1_.1, s32[1,2048]{1,0:T(1,128)} %bitcast.7, s32[8,128]{1,0:T(8,128)} %bitcast.9, s32[1,2048]{1,0:T(1,128)} %bitcast.8, bf16[768,512]{1,0:T(8,128)(2,1)} %refs_5_.1, ...), custom_call_target="tpu_custom_call" | custom-call | tf_op jit(solution)/shard_map/pallas_call | solution.py:427
  64.9 25.2 %shard_map.122 = (f32[1,2048]{1,0:T(1,128)}, f32[192,512]{1,0:T(8,128)}, f32[192,512]{1,0:T(8,128)}) custom-call(f32[1,2048]{1,0:T(1,128)} %get-tuple-element.9.refs_0_, f32[192,512]{1,0:T(8,128)} %get-tuple-element.10.refs_1_, f32[192,512]{1,0:T(8,128)} %get-tuple-element.11.refs_2_), custom_call_target="tpu_custom_call" | custom-call | tf_op jit(solution)/shard_map/pallas_call | solution.py:445

commit v2 on v1

--- a/solution.py
+++ b/solution.py
@@ -144,8 +144,11 @@
         for p in range(step // each):
             out_ref[c * (step // each) + p] = got[:, p * each:(p + 1) * each]
     pl.semaphore_wait(barrier, parts + slices - 2)
-    for j in range(1, parts):
-        dom_copy(0, j, out_ref.at[dom_peer(j)], inc_ref.at[d])
+    cuts = 2 if cols % 32 == 0 else 1
+    bands = [slice(c * cols // cuts, (c + 1) * cols // cuts) for c in range(cuts)]
+    for c, band in enumerate(bands):
+        for j in range(1, parts):
+            dom_copy(7 * c, j, out_ref.at[dom_peer(j), band], inc_ref.at[d, band])
     inc_ref[d] = out_ref[d]
 
     for j in far_first:
@@ -188,7 +191,8 @@
     def count_block(index):
         lax.fori_loop(0, block // 128, count_lanes, index * block)
 
-    for j in far_first:
+    far = far_first[:-1]
+    for j in far:
         count_block(feat_peer(j))
     inverse = 1.0 / degree_ref[...].astype(F32)
 
@@ -197,25 +201,30 @@
     for k, ref in enumerate((bias_ref, as_ref, an_ref)):
         col_ref[k] = jnp.broadcast_to(ref[...], (128, hid)).T
 
-    for j in range(1, parts):
-        dom_wait(0, j, inc_ref.at[dom_from(j)])
-    for p in range(parts):
-        inctab_ref[:, p * each:(p + 1) * each] = inc_ref[p]
-
     tile = min(256, block)
 
-    def aggregate(index):
+    def aggregate(index, band):
         for t in range(block // tile):
             lanes = pl.ds(pl.multiple_of(index * block + t * tile, tile), tile)
-            sums = dot(feat_ref[...], count_ref[:nodes, lanes], NN)
-            sums = sums + dot(inctab_ref[...], count_ref[nodes:, lanes], NN)
-            agg_ref[:, lanes] = (sums * (1.0 / degree_ref[:, lanes].astype(F32))).astype(BF)
-
-    for j in far_first:
-        aggregate(feat_peer(j))
-        feat_copy(1, j, agg_ref.at[:, span(feat_peer(j))], ablk_ref.at[f])
+            sums = dot(feat_ref[band, :], count_ref[:nodes, lanes], NN)
+            sums = sums + dot(inctab_ref[band, :], count_ref[nodes:, lanes], NN)
+            agg_ref[band, lanes] = (sums * (1.0 / degree_ref[:, lanes].astype(F32))).astype(BF)
+
+    for c, band in enumerate(bands):
+        if c == cuts - 1:
+            count_block(feat_peer(1))
+        for j in range(1, parts):
+            dom_wait(7 * c, j, inc_ref.at[dom_from(j), band])
+        for p in range(parts):
+            inctab_ref[band, p * each:(p + 1) * each] = inc_ref[p, band]
+        for j in far:
+            aggregate(feat_peer(j), band)
+            feat_copy(1 + 3 * c, j, agg_ref.at[band, span(feat_peer(j))], ablk_ref.at[f, band])
+    whole_band = slice(0, cols)
+    aggregate(feat_peer(1), whole_band)
+    feat_copy(1, 1, agg_ref.at[:, span(feat_peer(1))], ablk_ref.at[f])
     count_block(f)
-    aggregate(f)
+    aggregate(f, whole_band)
     ablk_ref[f] = agg_ref[:, span(f)]
 
     for j in range(1, slices):
@@ -226,8 +235,10 @@
     wt_ref[0] = ws_ref[...].T
     wt_ref[1] = wn_ref[...].T
     pre_ref[...] = dot(wt_ref[0], fblk_ref[...].reshape(depth, block), NN)
-    for j in range(1, slices):
-        feat_wait(1, j, ablk_ref.at[feat_from(j)])
+    feat_wait(1, 1, ablk_ref.at[feat_from(1)])
+    for c, band in enumerate(bands):
+        for j in far:
+            feat_wait(1 + 3 * c, j, ablk_ref.at[feat_from(j), band])
     pre_ref[...] += dot(wt_ref[1], ablk_ref[...].reshape(depth, block), NN)
     for t in range(block // 128):
         pre = pre_ref[:, t * 128:(t + 1) * 128] + col_ref[0]
@@ -368,7 +379,7 @@
             for j in range(1, parts, 2):
                 dom_wait(5 + h, j, ag_ref.at[h, lax.rem(beside + parts + 1 - j, parts)])
             for p in range(parts):
-                ref[spots[p][0], spots[p][1]] = ag_ref[h, p].astype(F32)
+                ref[spots[p][0], spots[p][1]] = ag_ref[h, p]
     else:
         gself_ref[...] = acc_ref[0]
         gneigh_ref[...] = acc_ref[1]
@@ -376,13 +387,10 @@
         copy.wait_send()
 
 
-def place(*refs):
-    sems = refs[6]
-    copies = [pltpu.make_async_copy(refs[k], refs[3 + k], sems.at[k]) for k in range(3)]
-    for copy in copies:
-        copy.start()
-    for copy in copies:
-        copy.wait()
+def place(logit_ref, gself_ref, gneigh_ref, logit_out, gself_out, gneigh_out):
+    logit_out[...] = logit_ref[...]
+    gself_out[...] = gself_ref[...].astype(F32)
+    gneigh_out[...] = gneigh_ref[...].astype(F32)
 
 
 def body(features, neighbors, degree, send_rows, labels, w_self, w_neigh, bias, a_self, a_neigh):
@@ -419,8 +427,8 @@
         V((2, cols, hid), F32), V((slices, hid, block), BF),
         V((2, parts, spare, hid // 2), BF), V((2, parts, spare, hid // 2), BF), V((2, parts, spare, hid // 2), BF),
         V((2, hid, w_self.shape[0]), BF),
-        pltpu.SemaphoreType.DMA((4, slices)), pltpu.SemaphoreType.DMA((4, slices)),
-        pltpu.SemaphoreType.DMA((7, parts)), pltpu.SemaphoreType.DMA((7, parts)),
+        pltpu.SemaphoreType.DMA((5, slices)), pltpu.SemaphoreType.DMA((5, slices)),
+        pltpu.SemaphoreType.DMA((8, parts)), pltpu.SemaphoreType.DMA((8, parts)),
         pltpu.SemaphoreType.DMA((10,)),
     ]
     vm = pl.BlockSpec(memory_space=pltpu.VMEM)
@@ -428,8 +436,8 @@
         functools.partial(kernel, parts, slices, reduce_here, scale),
         out_shape=(
             jax.ShapeDtypeStruct((1, nodes), F32),
-            jax.ShapeDtypeStruct((cols, hid), F32),
-            jax.ShapeDtypeStruct((cols, hid), F32),
+            jax.ShapeDtypeStruct((cols, hid), BF if reduce_here else F32),
+            jax.ShapeDtypeStruct((cols, hid), BF if reduce_here else F32),
         ),
         in_specs=[pl.BlockSpec(memory_space=pltpu.HBM)] * 10,
         out_specs=(vm, vm, vm),
@@ -441,13 +449,11 @@
         w_self, w_neigh, bias.reshape(1, hid), a_self.reshape(1, hid), a_neigh.reshape(1, hid),
     )
     if reduce_here:
-        hbm = pl.BlockSpec(memory_space=pltpu.HBM)
         logits, grad_self, grad_neigh = pl.pallas_call(
             place,
-            out_shape=tuple(jax.ShapeDtypeStruct(x.shape, x.dtype) for x in (logits, grad_self, grad_neigh)),
-            in_specs=[hbm] * 3,
-            out_specs=(hbm, hbm, hbm),
-            scratch_shapes=[pltpu.SemaphoreType.DMA((3,))],
+            out_shape=tuple(jax.ShapeDtypeStruct(x.shape, F32) for x in (logits, grad_self, grad_neigh)),
+            in_specs=[vm] * 3,
+            out_specs=(vm, vm, vm),
             compiler_params=pltpu.CompilerParams(vmem_limit_bytes=62 * 1024 * 1024),
         )(logits, grad_self, grad_neigh)
     else:

time: 90.4 us -> 67.2 us (0.74)
  Pallas kernels: 89.5 us -> 66.4 us
    pallas_call x1, Pallas kernels: 25.2 us -> 1.94 us  [body(): pl.pallas_call(place, out_shape=tuple((jax.ShapeDtypeStruct(x.shape, F32)...]
where the time goes in v2:
time: 67.2 us; the launch traced here: 67 us
  Pallas kernels  66.4 us (99%)
    pallas_call x1, Pallas kernels, body(): pl.pallas_call(functools.partial(kernel, parts, slices, reduce_here, scal...  64.4 us
    pallas_call x1, Pallas kernels, body(): pl.pallas_call(place, out_shape=tuple((jax.ShapeDtypeStruct(x.shape, F32)...  1.94 us

profile of v2, /device:TPU:0, one launch (start us, length us, event | category | flops | bytes accessed | tf_op | source)
XLA Modules:
  0.0 67.0 jit_solution(10129131899302490387)
XLA Ops:
  0.6 64.4 %shard_map.121 = (f32[1,2048]{1,0:T(1,128)}, bf16[192,512]{1,0:T(8,128)(2,1)}, bf16[192,512]{1,0:T(8,128)(2,1)}) custom-call(bf16[192,2048]{1,0:T(8,128)(2,1)} %refs_0_.1, s32[16,2048]{1,0:T(8,128)} %refs_1_.1, s32[1,2048]{1,0:T(1,128)} %bitcast.7, s32[8,128]{1,0:T(8,128)} %bitcast.9, s32[1,2048]{1,0:T(1,128)} %bitcast.8, bf16[768,512]{1,0:T(8,128)(2,1)} %refs_5_.1, ...), custom_call_target="tpu_custom_call" | custom-call | tf_op jit(solution)/shard_map/pallas_call | solution.py:435
  65.1 1.9 %shard_map.122 = (f32[1,2048]{1,0:T(1,128)}, f32[192,512]{1,0:T(8,128)}, f32[192,512]{1,0:T(8,128)}) custom-call(f32[1,2048]{1,0:T(1,128)} %get-tuple-element.9.logit_ref, bf16[192,512]{1,0:T(8,128)(2,1)} %get-tuple-element.10.gself_ref, bf16[192,512]{1,0:T(8,128)(2,1)} %get-tuple-element.11.gneigh_ref), custom_call_target="tpu_custom_call" | custom-call | tf_op jit(solution)/shard_map/pallas_call | solution.py:452

commit v3 on v2

--- a/solution.py
+++ b/solution.py
@@ -49,7 +49,7 @@
     logit_ref, gself_ref, gneigh_ref,
     hi_ref, val_ref, count_ref, pick_ref, fblk_ref, ablk_ref, agg_ref, out_ref, inc_ref, inctab_ref,
     col_ref, pre_ref, mask_ref, score_ref, srow_ref, sout_ref, sin_ref, stab_ref, wsplit_ref, slot_ref,
-    gout_ref, gin_ref, back_ref, dn_ref, dl_ref, acc_ref, dpre_ref, rs_out, rs_in, ag_ref, wt_ref,
+    gout_ref, gin_ref, back_ref, dn_ref, dl_ref, acc_ref, dpre_ref, rs_out, rs_in, ag_ref, rs_mid, rs_got, wt_ref,
     feat_send, feat_recv, dom_send, dom_recv, load_sem,
 ):
     feat_ref, neigh_ref, degree_ref, send_ref, label_ref, ws_ref, wn_ref, bias_ref, as_ref, an_ref = held
@@ -169,8 +169,8 @@
         base = lax.broadcasted_iota(jnp.int32, (8, 128), 0)
 
         def count_rows(i, _):
-            for u in range(0, 32, 16):
-                r = pl.multiple_of(i * 32 + u, 16)
+            for u in range(0, 64, 16):
+                r = pl.multiple_of(i * 64 + u, 16)
                 words = []
                 for here in (base + r, base + (r + 8)):
                     terms = [jnp.where(h == here, v, 0) for h, v in zip(his, vals)]
@@ -185,7 +185,7 @@
                     count_ref[pl.ds(pl.multiple_of(g * rows + r, 16), 16), lanes] = both.astype(BF)
             return 0
 
-        lax.fori_loop(0, rows // 32, count_rows, 0)
+        lax.fori_loop(0, rows // 64, count_rows, 0)
         return first
 
     def count_block(index):
@@ -338,11 +338,21 @@
     share = 2 * cols // parts
     spots = [(slice(p // 2 * share, (p // 2 + 1) * share), slice(p % 2 * half, (p % 2 + 1) * half)) for p in range(parts)]
 
+    beside = d + 1 - 2 * lax.rem(d, 2)
+
+    def to_beside(phase, j, src, dst):
+        copy = pltpu.make_async_remote_copy(
+            src_ref=src, dst_ref=dst, send_sem=dom_send.at[phase, j], recv_sem=dom_recv.at[phase, j],
+            device_id={"dom": beside}, device_id_type=MESH)
+        copy.start()
+        sent.append(copy)
+
     def send_shares(h):
         for p in range(parts):
             rs_out[h, p] = acc_ref[h, spots[p][0], spots[p][1]].astype(BF)
-        for j in range(1, parts):
-            dom_copy(3 + h, j, rs_out.at[h, dom_peer(j)], rs_in.at[h, d])
+        for j in list(range(2, parts, 2)) + [0]:
+            index = lax.rem(beside + j, parts)
+            to_beside(3 + h, j + 1, rs_out.at[h, index], rs_in.at[h, index])
 
     if reduce_here:
         send_shares(0)
@@ -351,30 +361,27 @@
         acc_ref[1] = acc_ref[1] + other if j else other
     if reduce_here:
         send_shares(1)
-        side = lax.rem(d, 2)
-        beside = d + 1 - 2 * side
-
-        def hand_over(h, j, index):
-            copy = pltpu.make_async_remote_copy(
-                src_ref=ag_ref.at[h, index], dst_ref=ag_ref.at[h, index],
-                send_sem=dom_send.at[5 + h, j], recv_sem=dom_recv.at[5 + h, j],
-                device_id={"dom": beside}, device_id_type=MESH)
-            copy.start()
-            sent.append(copy)
-
         for h in range(2):
-            whole = rs_out[h, d].astype(F32)
-            for j in range(1, parts):
-                dom_wait(3 + h, j, rs_in.at[h, dom_from(j)])
-                whole = whole + rs_in[h, dom_from(j)].astype(F32)
+            for j in range(2, parts, 2):
+                index = dom_peer(j)
+                dom_wait(3 + h, j + 1, rs_in.at[h, index])
+                pair = rs_out[h, index].astype(F32) + rs_in[h, index].astype(F32)
+                rs_mid[h, index] = pair.astype(BF)
+                dom_copy(3 + h, j, rs_mid.at[h, index], rs_got.at[h, d])
+        for h in range(2):
+            dom_wait(3 + h, 1, rs_in.at[h, d])
+            whole = rs_out[h, d].astype(F32) + rs_in[h, d].astype(F32)
+            for j in range(2, parts, 2):
+                dom_wait(3 + h, j, rs_got.at[h, dom_from(j)])
+                whole = whole + rs_got[h, dom_from(j)].astype(F32)
             ag_ref[h, d] = whole.astype(BF)
             for j in range(2, parts, 2):
                 dom_copy(5 + h, j, ag_ref.at[h, d], ag_ref.at[h, d])
-            hand_over(h, 1, d)
+            to_beside(5 + h, 1, ag_ref.at[h, d], ag_ref.at[h, d])
         for h in range(2):
             for j in range(2, parts, 2):
                 dom_wait(5 + h, j, ag_ref.at[h, dom_from(j)])
-                hand_over(h, j + 1, dom_from(j))
+                to_beside(5 + h, j + 1, ag_ref.at[h, dom_from(j)], ag_ref.at[h, dom_from(j)])
         for h, ref in enumerate((gself_ref, gneigh_ref)):
             for j in range(1, parts, 2):
                 dom_wait(5 + h, j, ag_ref.at[h, lax.rem(beside + parts + 1 - j, parts)])
@@ -425,7 +432,7 @@
         V((parts, 8, each), F32), V((parts, 8, each), F32), V((8, remote), F32),
         V((8, nodes), F32), V((1, nodes), F32),
         V((2, cols, hid), F32), V((slices, hid, block), BF),
-        V((2, parts, spare, hid // 2), BF), V((2, parts, spare, hid // 2), BF), V((2, parts, spare, hid // 2), BF),
+        *[V((2, parts, spare, hid // 2), BF)] * 5,
         V((2, hid, w_self.shape[0]), BF),
         pltpu.SemaphoreType.DMA((5, slices)), pltpu.SemaphoreType.DMA((5, slices)),
         pltpu.SemaphoreType.DMA((8, parts)), pltpu.SemaphoreType.DMA((8, parts)),

time: 67.2 us -> 65 us (0.967)
  Pallas kernels: 66.4 us -> 64.2 us
    pallas_call x1, Pallas kernels: 64.4 us -> 62.3 us  [body(): pl.pallas_call(functools.partial(kernel, parts, slices, reduce_here, scal...]
where the time goes in v3:
time: 65 us; the launch traced here: 64.9 us
  Pallas kernels  64.2 us (99%)
    pallas_call x1, Pallas kernels, body(): pl.pallas_call(functools.partial(kernel, parts, slices, reduce_here, scal...  62.3 us
    pallas_call x1, Pallas kernels, body(): pl.pallas_call(place, out_shape=tuple((jax.ShapeDtypeStruct(x.shape, F32)...  1.94 us

profile of v3, /device:TPU:0, one launch (start us, length us, event | category | flops | bytes accessed | tf_op | source)
XLA Modules:
  0.0 64.9 jit_solution(173791835907314802)
XLA Ops:
  0.6 62.3 %shard_map.121 = (f32[1,2048]{1,0:T(1,128)}, bf16[192,512]{1,0:T(8,128)(2,1)}, bf16[192,512]{1,0:T(8,128)(2,1)}) custom-call(bf16[192,2048]{1,0:T(8,128)(2,1)} %refs_0_.1, s32[16,2048]{1,0:T(8,128)} %refs_1_.1, s32[1,2048]{1,0:T(1,128)} %bitcast.7, s32[8,128]{1,0:T(8,128)} %bitcast.9, s32[1,2048]{1,0:T(1,128)} %bitcast.8, bf16[768,512]{1,0:T(8,128)(2,1)} %refs_5_.1, ...), custom_call_target="tpu_custom_call" | custom-call | tf_op jit(solution)/shard_map/pallas_call | solution.py:442
  62.9 1.9 %shard_map.122 = (f32[1,2048]{1,0:T(1,128)}, f32[192,512]{1,0:T(8,128)}, f32[192,512]{1,0:T(8,128)}) custom-call(f32[1,2048]{1,0:T(1,128)} %get-tuple-element.9.logit_ref, bf16[192,512]{1,0:T(8,128)(2,1)} %get-tuple-element.10.gself_ref, bf16[192,512]{1,0:T(8,128)(2,1)} %get-tuple-element.11.gneigh_ref), custom_call_target="tpu_custom_call" | custom-call | tf_op jit(solution)/shard_map/pallas_call | solution.py:459
